TPU v7x, 256 devices: a whole 4x4x8 slice. The times are simulated.
256 devices in a mesh: dom: 64 (over y, z, core), sub: 4 (over x).
Axes of the slice: x: 4, y: 4, z: 8, core: 2. Of those that a mesh axis runs over, the one named last changes fastest.
Arguments:
- a_blocks: bfloat16 [4096, 64, 448], P(('dom', 'sub')), may hold values from -0.25 to 0.25
- a_nbrs: int32 [4096, 6], P(('dom', 'sub')), may hold values from 0 to 143
- p_blocks: bfloat16 [4096, 64, 128], P(('dom', 'sub')), may hold values from -3 to 3
- p_dest: int32 [4096, 1], P(('dom', 'sub')), may hold values from 0 to 63; in each aligned block of 16 rows (0 to 15, 16 to 31, ...) at most 2 rows name the same one
- p_far_agg: int32 [4096, 1], P(('dom', 'sub')), may hold values from 0 to 1
- agg_id: int32 [256, 16], P(('dom', 'sub')), may hold values from 0 to 1, never falling along the last dimension, each value on 1 to 15 neighbouring positions
- ap_slot: int32 [4096, 7, 2], P(('dom', 'sub')), may hold values from 0 to 7
- c_slot: int32 [4096, 2, 8], P(('dom', 'sub')), may hold values from 0 to 5
- send_rows: int32 [16384, 2], P(('dom', 'sub')), may hold values from 0 to 15
Outputs:
- coarse: bfloat16 [512, 64, 384], P('dom')
Inputs may be any that keep to these rules, and one draw needn't show every extreme that they name: `a_nbrs`: entries below 16 are rows of the same device; entry 16 + p * 2 + f is the f-th row sent by device p of the same sub index. `p_dest`: among one device's 16 rows no dom index is named by more than 2 rows, and some device's rows reach that bound. `agg_id`: never falling along a device's rows; each aggregate holds 1 to 15 rows.
All inputs are finite; a program needn't handle non-finite values.
Results may differ from a plain program's by a relative error of at most 0.005.
Values may be sent and summed in bfloat16 or wider, within the bound.
A program may use at most 192 MiB of HBM per device.

v0:
```python
import jax
import jax.numpy as jnp
from jax import lax
from jax.sharding import PartitionSpec as P

KA = 7
KP = 2
KAP = 8
KC = 6
AGG_DEV = 2


def place_blocks(coarse_sum, contrib, targets):
    item_count = contrib.shape[0]
    coarse_width = contrib.shape[1]
    blocks = contrib.reshape(item_count, coarse_width, -1, coarse_width).transpose(0, 2, 1, 3)
    blocks = blocks.reshape(-1, coarse_width, coarse_width)
    return coarse_sum.at[targets.reshape(-1)].add(blocks, mode="drop")


def body(a_blocks, a_nbrs, p_blocks, p_dest, p_far_agg, agg_id, ap_slot, c_slot, send_rows):
    row_count = a_blocks.shape[0]
    fine_width = a_blocks.shape[1]
    coarse_width = p_blocks.shape[2] // KP
    peer_count = lax.axis_size("dom")
    fetch_slots = send_rows.shape[1]
    return_slots = max(2, 2 * row_count // peer_count)
    outgoing = p_blocks[send_rows]
    received = lax.all_to_all(outgoing, "dom", split_axis=0, concat_axis=0, tiled=True)
    extended = jnp.concatenate(
        [p_blocks, received.reshape(peer_count * fetch_slots, fine_width, KP * coarse_width)],
        axis=0,
    )
    local_iota = jnp.arange(row_count, dtype=jnp.int32)
    columns = jnp.concatenate([local_iota[:, None], a_nbrs], axis=1)
    gathered = extended[columns]
    product = jnp.einsum(
        "rbke,rkec->rkbc",
        a_blocks.reshape(row_count, fine_width, KA, fine_width),
        gathered,
        preferred_element_type=jnp.float32,
    )
    select = (ap_slot[..., None] == jnp.arange(KAP, dtype=jnp.int32)).astype(jnp.float32)
    merged = jnp.einsum(
        "rkblc,rklq->rbqc",
        product.reshape(row_count, KA, fine_width, KP, coarse_width),
        select,
        precision=lax.Precision.HIGHEST,
    )
    merged = merged.reshape(row_count, fine_width, KAP * coarse_width).astype(jnp.bfloat16)
    p_four = p_blocks.reshape(row_count, fine_width, KP, coarse_width)
    empty_slot = AGG_DEV * KC
    near_slots = agg_id[0][:, None] * KC + c_slot[:, 0, :]
    one_hot = (p_dest == jnp.arange(peer_count, dtype=jnp.int32)[None, :]).astype(jnp.int32)
    before = jnp.cumsum(one_hot, axis=0) - one_hot
    position = jnp.sum(before * one_hot, axis=1)
    placing = p_dest[:, 0] * return_slots + position
    meta_rows = jnp.concatenate([p_far_agg, c_slot[:, 1, :]], axis=1).astype(jnp.float32)

    def to_buffer(values, fill_value):
        shaped = jnp.full((peer_count * return_slots,) + values.shape[1:], fill_value, values.dtype)
        shaped = shaped.at[placing].set(values)
        return shaped.reshape((peer_count, return_slots) + values.shape[1:])

    coarse_sum = jnp.zeros((AGG_DEV * KC, coarse_width, coarse_width), jnp.float32)
    contrib = jnp.einsum("rbmc,rbx->rmcx", p_four, merged, preferred_element_type=jnp.float32)
    coarse_sum = place_blocks(coarse_sum, contrib[:, 0], near_slots)
    far_block, far_meta = (
        lax.all_to_all(
            to_buffer(contrib[:, 1], 0.0), "dom", split_axis=0, concat_axis=0, tiled=True
        ),
        lax.all_to_all(to_buffer(meta_rows, -1.0), "dom", split_axis=0, concat_axis=0, tiled=True),
    )
    far_block = far_block.reshape(-1, coarse_width, KAP * coarse_width)
    far_meta = far_meta.reshape(-1, KAP + 1)
    far_valid = far_meta[:, 0] >= 0.0
    far_slots = jnp.where(
        far_valid[:, None],
        far_meta[:, 0:1].astype(jnp.int32) * KC + far_meta[:, 1:].astype(jnp.int32),
        empty_slot,
    )
    coarse_sum = place_blocks(coarse_sum, far_block, far_slots)
    coarse = coarse_sum.reshape(AGG_DEV, KC, coarse_width, coarse_width).transpose(0, 2, 1, 3)
    coarse = coarse.reshape(AGG_DEV, coarse_width, KC * coarse_width).astype(jnp.bfloat16)
    return lax.all_gather(coarse, "sub", axis=0, tiled=True)


def solution(mesh):
    return jax.shard_map(
        body,
        mesh=mesh,
        in_specs=(
            P(("dom", "sub"), None, None),
            P(("dom", "sub"), None),
            P(("dom", "sub"), None, None),
            P(("dom", "sub"), None),
            P(("dom", "sub"), None),
            P(("dom", "sub"), None),
            P(("dom", "sub"), None, None),
            P(("dom", "sub"), None, None),
            P(("dom", "sub"), None),
        ),
        out_specs=P("dom", None, None),
        check_vma=False,
    )
```

profile of v0, /device:TPU:1, one launch (start us, length us, event | category | flops | bytes accessed | tf_op | source)
XLA Modules:
  0.0 663.7 jit_solution(5790746913374935227)
XLA Ops:
  0.0 0.7 compare_select_fusion.2
  0.8 0.1 reshape.181
  0.9 3.1 gather_fusion
  4.1 13.3 %all-to-all-start = ((bf16[64,2,64,128]{3,2,1,0:T(8,128)(2,1)}), bf16[64,2,64,128]{3,2,1,0:T(8,128)(2,1)S(1)}, u32[]{:S(2)}, u32[]{:S(2)}) async-start(bf16[64,2,64,128]{3,2,1,0:T(8,128)(2,1)} %bitcast.74), calls=%async_computation | async-start | bytes 4194304 | tf_op jit(solution)/shard_map/all_to_all | solution.py:29
  17.8 2.3 reshape.170
  20.2 0.2 select_reduce_fusion
  20.4 1.2 scatter_custom_fusion.1
  21.7 47.0 %all-to-all-done = bf16[64,2,64,128]{3,2,1,0:T(8,128)(2,1)S(1)} async-done(((bf16[64,2,64,128]{3,2,1,0:T(8,128)(2,1)}), bf16[64,2,64,128]{3,2,1,0:T(8,128)(2,1)S(1)}, u32[]{:S(2)}, u32[]{:S(2)}) %all-to-all-start) | async-done | bytes 2097184 | tf_op jit(solution)/shard_map/all_to_all | solution.py:29
  68.6 5.8 all-to-all-start.1
  74.5 1.6 pad_maximum_fusion
  76.1 3.9 gather_fusion.1
  80.0 4.0 convolution_bitcast_fusion
  84.0 8.3 %reshape.171 = f32[16,7,64,2,64]{4,3,2,1,0:T(2,128)} reshape(f32[16,7,64,128]{3,2,1,0:T(8,128)} %convolution_bitcast_fusion) | data formatting | bytes 7340032 | tf_op jit(solution)/shard_map/reshape | solution.py:46
  92.3 10.4 %fusion.5 = bf16[16,64,8,64]{3,2,1,0:T(8,128)(2,1)S(1)} fusion(f32[16,7,64,2,64]{4,3,2,1,0:T(2,128)} %reshape.171, s32[16,7,2]{1,2,0:T(2,128)S(1)} %copy.39), kind=kOutput, calls=%fused_computation.13 | convolution fusion | flops 88606464 | bytes 4719488 | tf_op jit(solution)/shard_map/rkblc,rklq->rbqc/dot_general | solution.py:44
  102.7 1.5 convert_element_type.36
  104.2 0.8 fusion.18
  105.0 2.0 slice_bitcast_fusion
  107.0 7.9 %broadcast_in_dim.42 = f32[128,64,512]{2,1,0:T(8,128)} broadcast(f32[]{:T(128)} %constant.9.clone.1), dimensions={} | broadcast | bytes 16777220 | tf_op jit(solution)/shard_map/broadcast_in_dim | solution.py:61
  114.8 4.5 scatter_fusion.1
  119.3 10.6 %all-to-all-start.2 = ((f32[64,2,64,512]{3,2,1,0:T(8,128)}), f32[64,2,64,512]{3,2,1,0:T(8,128)}, u32[]{:S(2)}, u32[]{:S(2)}) async-start(f32[64,2,64,512]{3,2,1,0:T(8,128)} %bitcast.70), calls=%async_computation.2 | async-start | bytes 33554432 | tf_op jit(solution)/shard_map/all_to_all | solution.py:69
  130.5 0.1 fusion.11
  130.8 2.4 reshape_squeeze.3
  133.1 4.9 copy.45
  138.1 13.6 %scatter_fusion = f32[12,64,64]{2,1,0:T(8,128)S(1)} fusion(f32[12,64,64]{2,1,0:T(8,128)S(1)} %broadcast_in_dim.36, s32[128]{0:T(128)S(1)} %fusion.16, f32[128,64,64]{2,1,0:T(8,128)} %bitcast.71), kind=kCustom, calls=%fused_computation.2 | custom fusion | flops 524288 | bytes 6291968 | tf_op jit(solution)/shard_map/scatter-add | solution.py:18
  151.6 343.8 %all-to-all-done.2 = f32[64,2,64,512]{3,2,1,0:T(8,128)} async-done(((f32[64,2,64,512]{3,2,1,0:T(8,128)}), f32[64,2,64,512]{3,2,1,0:T(8,128)}, u32[]{:S(2)}, u32[]{:S(2)}) %all-to-all-start.2) | async-done | bytes 16777248 | tf_op jit(solution)/shard_map/all_to_all | solution.py:69
  495.5 24.7 %reshape_reshape.3 = f32[128,64,8,64]{3,2,1,0:T(8,128)} reshape(f32[64,2,64,512]{3,2,1,0:T(8,128)} %all-to-all-done.2) | data formatting | bytes 33554432 | tf_op jit(solution)/shard_map/reshape;reshape | solution.py:16
  520.1 27.5 %copy.47 = f32[128,8,64,64]{3,2,1,0:T(8,128)} copy(f32[128,8,64,64]{3,1,2,0:T(8,128)} %bitcast.69) | data formatting | bytes 33554432 | tf_op jit(solution)/shard_map/transpose | solution.py:16
  547.7 104.0 %scatter_fusion.2 = f32[12,64,64]{2,1,0:T(8,128)S(1)} fusion(f32[12,64,64]{2,1,0:T(8,128)S(1)} %scatter_fusion, s32[1024]{0:T(1024)S(1)} %bitcast.80, f32[1024,64,64]{2,1,0:T(8,128)} %bitcast.68), kind=kCustom, calls=%fused_computation.5 | custom fusion | flops 4194304 | bytes 50335744 | tf_op jit(solution)/shard_map/scatter-add | solution.py:18
  651.7 0.1 copy.48
  651.8 0.2 convert_element_type.44
  652.0 11.0 %all_gather.3 = bf16[8,64,384]{2,1,0:T(8,128)(2,1)S(1)} all-gather(bf16[2,64,384]{2,1,0:T(8,128)(2,1)S(1)} %convert_element_type.44), channel_id=1, replica_groups=mesh['dom'=64,'sub'=4] {'sub'}, dimensions={0}, use_global_device_ids=true | all-gather | bytes 491520 | tf_op jit(solution)/shard_map/all_gather | solution.py:85
  663.0 0.7 copy.64
  (45 shorter events, 1.4 us)
Async XLA Ops:
  4.1 13.4 %copy-start.5 = (s32[16,6]{0,1:T(8,128)S(1)}, s32[16,6]{0,1:T(8,128)}, u32[]{:S(2)}) copy-start(s32[16,6]{0,1:T(8,128)} %param.10) | copy-start | bytes 1156
  4.1 13.6 %copy-start.3 = (s32[16,2,8]{0,2,1:T(8,128)S(1)}, s32[16,2,8]{0,2,1:T(8,128)}, u32[]{:S(2)}) copy-start(s32[16,2,8]{0,2,1:T(8,128)} %param.16) | copy-start | bytes 3076
  4.1 13.6 %copy-start.7 = (s32[16,1]{0,1:T(1,128)S(1)}, s32[16,1]{0,1:T(1,128)}, u32[]{:S(2)}) copy-start(s32[16,1]{0,1:T(1,128)} %param.13) | copy-start | bytes 196
  4.1 13.7 %copy-start.4 = (s32[16,7,2]{0,2,1:T(2,128)S(1)}, s32[16,7,2]{0,2,1:T(2,128)}, u32[]{:S(2)}) copy-start(s32[16,7,2]{0,2,1:T(2,128)} %param.15) | copy-start | bytes 2692
  4.1 13.8 %copy-start.2 = (bf16[16,64,448]{2,1,0:T(8,128)(2,1)S(1)}, bf16[16,64,448]{2,1,0:T(8,128)(2,1)}, u32[]{:S(2)}) copy-start(bf16[16,64,448]{2,1,0:T(8,128)(2,1)} %param.9) | copy-start | bytes 2752516
  4.1 64.6 %all-to-all-start = ((bf16[64,2,64,128]{3,2,1,0:T(8,128)(2,1)}), bf16[64,2,64,128]{3,2,1,0:T(8,128)(2,1)S(1)}, u32[]{:S(2)}, u32[]{:S(2)}) async-start(bf16[64,2,64,128]{3,2,1,0:T(8,128)(2,1)} %bitcast.74), calls=%async_computation | async-start | bytes 4194304 | tf_op jit(solution)/shard_map/all_to_all | solution.py:29
  17.4 2.7 copy-start.6
  17.4 57.1 %copy-start = (bf16[16,64,128]{2,1,0:T(8,128)(2,1)S(1)}, bf16[16,64,128]{2,1,0:T(8,128)(2,1)}, u32[]{:S(2)}) copy-start(bf16[16,64,128]{2,1,0:T(8,128)(2,1)} %param.11) | copy-start | bytes 786436
  68.6 50.7 %all-to-all-start.1 = ((f32[64,2,9]{2,1,0:T(2,128)}), f32[64,2,9]{2,1,0:T(2,128)S(1)}, u32[]{:S(2)}, u32[]{:S(2)}) async-start(f32[64,2,9]{2,1,0:T(2,128)} %bitcast.22), calls=%async_computation.1 | async-start | bytes 131072 | tf_op jit(solution)/shard_map/all_to_all | solution.py:72
  76.1 3.9 copy-start.1
  119.3 10.6 %copy-start.8 = (s32[1,16]{1,0:T(1,128)S(1)}, s32[1,16]{1,0:T(1,128)}, u32[]{:S(2)}) copy-start(s32[1,16]{1,0:T(1,128)} %param.14) | copy-start | bytes 196
  119.3 376.2 %all-to-all-start.2 = ((f32[64,2,64,512]{3,2,1,0:T(8,128)}), f32[64,2,64,512]{3,2,1,0:T(8,128)}, u32[]{:S(2)}, u32[]{:S(2)}) async-start(f32[64,2,64,512]{3,2,1,0:T(8,128)} %bitcast.70), calls=%async_computation.2 | async-start | bytes 33554432 | tf_op jit(solution)/shard_map/all_to_all | solution.py:69
where the time goes:
time: 669 us; the launch traced here: 664 us
  waiting for transfers between devices  391 us (58%)
  other arithmetic  121 us (18%)
  local copies, waits for them, and re-layouts  96.2 us (14%)
  starting transfers between devices  29.8 us (4%)
  matrix products  15.2 us (2%)
  blocking collectives  11 us (2%)
    all_to_all x1, waiting for transfers between devices, body(): lax.all_to_all(to_buffer(contrib[:, 1], 0.0), 'dom', split_axis=0, concat...  344 us
    scatter-add x2, other arithmetic, place_blocks(): return coarse_sum.at[targets.reshape(-1)].add(blocks, mode='drop')  118 us
    all_to_all x1, waiting for transfers between devices, body(): lax.all_to_all(outgoing, 'dom', split_axis=0, concat_axis=0, tiled=True)  47 us
    another operation x3, local copies, waits for them, and re-layouts, place_blocks(): contrib.reshape(item_count, coarse_width, -1, coarse_width)  31.9 us
    transpose x1, local copies, waits for them, and re-layouts, place_blocks(): contrib.reshape(item_count, coarse_width, -1, coarse_width)  27.5 us
  transfers between devices with their start and end apart: 3, of which 2 were waited for; matrix products, arithmetic and copies ran while one was open for 11% of the time, Pallas kernels for 0%

commit v1 on v0

v1 whole, which is shorter than its diff:
```python
import functools

import jax
import jax.numpy as jnp
from jax import lax
from jax.experimental import pallas as pl
from jax.experimental.pallas import tpu as pltpu
from jax.sharding import PartitionSpec as P

MESH = pl.DeviceIdType.MESH
NZ = 8
NC = 2
R = 16
KA = 7
B = 64
AGG = 2
KC = 6
CHUNK = 8
f32, bf16, i32 = jnp.float32, jnp.bfloat16, jnp.int32


def kernel(ny, nx, nbr_s, dest_s, far_s, agg_s, slot_s, cslot_s, send_s, a_hbm, p_ref, out_ref, *scr):
    nz, nc = NZ, NC
    half = nz // 2
    nyc = ny * nc
    ml = B // nyc
    tr = nyc * AGG
    sl = ml * R
    near_rows = ml * AGG
    scr = list(scr)
    zr = [scr.pop(0) for _ in range(half - 1)]
    zl = [scr.pop(0) for _ in range(half - 1)]
    (zfar, a_vm, idx_out, idx_in, idx_s, cols_s, picks, ext, wbuf, near, wsend, r1, meta_out, meta_in, zsend, r2, total, osend, r3,
     a_sem, s_ring, r_ring, s_idx, r_idx, l_idx, s_pick, r_pick, s_one, r_one, s_meta, r_meta, s_two, r_two, s_three, r_three) = scr

    dom, x = lax.axis_index("dom"), lax.axis_index("sub")
    y = lax.div(dom, nz * nc)
    z = lax.rem(lax.div(dom, nc), nz)
    c = lax.rem(dom, nc)
    j = y * nc + c

    def along_z(step):
        return ((y * nz + lax.rem(z + step + nz, nz)) * nc + c, x)

    def in_plane(peer, px):
        return ((lax.div(peer, nc) * nz + z) * nc + lax.rem(peer, nc), px)

    def remote(src, dst, send, recv, device):
        return pltpu.make_async_remote_copy(
            src_ref=src, dst_ref=dst, send_sem=send, recv_sem=recv, device_id=device, device_id_type=MESH
        )

    def loop(lo, hi, fn):
        lax.fori_loop(lo, hi, lambda t, carry: (fn(t), carry)[1], 0)

    a_copy = pltpu.make_async_copy(a_hbm, a_vm, a_sem)
    a_copy.start()

    barrier = pltpu.get_barrier_semaphore()
    group = nx * nyc
    place = x * nyc + j
    loop(1, nz, lambda t: pl.semaphore_signal(barrier, inc=1, device_id=along_z(t), device_id_type=MESH))

    def greet(t):
        q = lax.rem(place + t, group)
        pl.semaphore_signal(barrier, inc=1, device_id=in_plane(lax.rem(q, nyc), lax.div(q, nyc)), device_id_type=MESH)

    loop(1, group, greet)
    pl.semaphore_wait(barrier, nz - 1 + group - 1)

    def ring(way, step, piece):
        there = (zr, zl)[way]
        src = p_ref if step == 1 else there[step - 2]
        dst = there[step - 1] if step < half else zfar
        rows = pl.ds(piece * CHUNK, CHUNK)
        return remote(
            src.at[rows], dst.at[rows], s_ring.at[way, step - 1, piece], r_ring.at[way, step - 1, piece],
            along_z(1 if way == 0 else -1),
        )

    pieces = R // CHUNK

    def order(way, step):
        listed = list(range(pieces)) if way == 0 else list(range(pieces))[::-1]
        return listed if step < half else listed[: pieces // 2]

    for piece in range(pieces):
        for way in (0, 1):
            ring(way, 1, order(way, 1)[piece]).start()

    lane = lax.broadcasted_iota(i32, (8, 128), 1)

    def list_for(t):
        zt = lax.rem(z + t, nz)
        tile = jnp.zeros((8, 128), i32)
        for peer in range(nyc):
            for f in range(2):
                row = send_s[((peer // nc) * nz + zt) * nc + peer % nc, f]
                tile = jnp.where(lane == peer * 2 + f, row, tile)
        return tile

    def slot_of(t):
        return 0 if t == 0 else 2 * t - 1 if t < half else nz - 1 if t == half else 2 * (nz - t)

    idx_in[0] = list_for(0)
    index_copies = []
    for t in range(1, nz):
        idx_out[t] = list_for(t)
        copy = remote(idx_out.at[t], idx_in.at[slot_of(t)], s_idx.at[t], r_idx.at[t], along_z(t))
        copy.start()
        index_copies.append(copy)

    def message(number):
        first = 0 if number == 0 else 2 * number - 1
        return first, (1 if number in (0, half) else 2)

    def pick_copy(number, t):
        first, count = message(number)
        return remote(
            picks.at[t, pl.ds(first * 2, count * 2)], ext.at[pl.ds(R + (j * nz + first) * 2, count * 2)],
            s_pick.at[number, t], r_pick.at[number, t], in_plane(lax.rem(j + t, nyc), x),
        )

    def pick(number, sources, index):
        first, count = message(number)
        for n, source in enumerate(sources):
            for f in range(2):
                ext[R + (j * nz + first + n) * 2 + f] = source[index(first + n, j, f)]

        def for_peer(t):
            peer = lax.rem(j + t, nyc)
            for n, source in enumerate(sources):
                for f in range(2):
                    picks[t, (first + n) * 2 + f] = source[index(first + n, peer, f)]
            pick_copy(number, t).start()

        loop(1, nyc, for_peer)

    pick(0, [p_ref], lambda slot, peer, f: send_s[(lax.div(peer, nc) * nz + z) * nc + lax.rem(peer, nc), f])
    ext[0:R] = p_ref[...]

    def place_row(i):
        cols_s[i * KA] = i
        for k in range(1, KA):
            n = nbr_s[i, k - 1]
            e = n - R
            f = e & 1
            owner = e >> 1
            oc = owner & (nc - 1)
            oz = (owner >> (nc.bit_length() - 1)) & (nz - 1)
            oy = owner >> ((nz * nc).bit_length() - 1)
            dz = (oz - z + nz) & (nz - 1)
            slot = jnp.where(dz == half, nz - 1, jnp.where(dz < half, 2 * dz, 2 * (nz - dz) - 1))
            cols_s[i * KA + k] = jnp.where(n < R, n, R + ((oy * nc + oc) * nz + slot) * 2 + f)

    loop(0, R, place_row)

    for copy in index_copies:
        copy.wait()
    to_scalars = pltpu.make_async_copy(idx_in, idx_s, l_idx)
    to_scalars.start()
    to_scalars.wait()
    listed = lambda slot, peer, f: idx_s[slot, 0, peer * 2 + f]

    for step in range(1, half + 1):
        for n in range(len(order(0, step))):
            for way in (0, 1):
                piece = order(way, step)[n]
                ring(way, step, piece).wait_recv()
                if step < half and piece in order(way, step + 1):
                    ring(way, step + 1, piece).start()
        pick(step, [zr[step - 1], zl[step - 1]] if step < half else [zfar], listed)
    for number in range(half + 1):
        loop(1, nyc, lambda t, number=number: pick_copy(number, t).wait_recv())
    a_copy.wait()

    lane1 = lax.broadcasted_iota(i32, (1, 128), 1)
    low = lane1 < B
    high = jnp.where(low, 0, 1)
    low_mask = jnp.where(low, 1.0, 0.0).astype(bf16)
    high_mask = jnp.where(low, 0.0, 1.0).astype(bf16)
    near[...] = jnp.zeros_like(near)

    def masks(s0, s1, pairs):
        same = jnp.where(low, s0, s1) - high
        cross = jnp.where(low, s1, s0) - high
        return [
            (jnp.where(same == 2 * q, 1.0, 0.0).astype(f32), jnp.where(cross == 2 * q, 1.0, 0.0).astype(f32))
            for q in range(pairs)
        ]

    def row(i):
        ap = [None] * 4

        def merge(k, q):
            turned = pltpu.roll(q, B, 1)
            for n, (same, cross) in enumerate(masks(slot_s[i, k, 0], slot_s[i, k, 1], 4)):
                term = q * same + turned * cross
                ap[n] = term if ap[n] is None else ap[n] + term

        for pair in range(KA // 2):
            a = a_vm[i, :, pair * 128:(pair + 1) * 128]
            left = jnp.concatenate([a * low_mask, a * high_mask], axis=0)
            right = jnp.concatenate([ext[cols_s[i * KA + 2 * pair]], ext[cols_s[i * KA + 2 * pair + 1]]], axis=0)
            q = jnp.dot(left, right, preferred_element_type=f32)
            merge(2 * pair, q[:B])
            merge(2 * pair + 1, q[B:])
        q = jnp.dot(a_vm[i, :, (KA - 1) * B:], ext[cols_s[i * KA + KA - 1]], preferred_element_type=f32)
        merge(KA - 1, q)
        merged = jnp.concatenate([block.astype(bf16) for block in ap], axis=1)
        w = lax.dot_general(p_ref[i], merged, (((0,), (0,)), ((), ())), preferred_element_type=f32)
        near_to, far_to = [None] * 3, [None] * 3
        for q in range(4):
            block = w[:, q * 128:(q + 1) * 128]
            turned = pltpu.roll(block, B, 1)
            for m, to in ((0, near_to), (1, far_to)):
                lines = slice(m * B, (m + 1) * B)
                for n, (same, cross) in enumerate(masks(cslot_s[i, m, 2 * q], cslot_s[i, m, 2 * q + 1], 3)):
                    term = block[lines] * same + turned[lines] * cross
                    to[n] = term if to[n] is None else to[n] + term
        agg = agg_s[0, i]
        for n in range(3):
            wbuf[n, pl.ds(i, B, stride=R), :] = far_to[n]
            for g in range(AGG):
                near[g, :, n * 128:(n + 1) * 128] += near_to[n] * jnp.where(agg == g, 1.0, 0.0).astype(f32)

    loop(0, R, row)

    meta = jnp.zeros((8, 128), i32)
    for i in range(R):
        d = dest_s[i, 0]
        dc = d & (nc - 1)
        dz = (d >> (nc.bit_length() - 1)) & (nz - 1)
        dy = d >> ((nz * nc).bit_length() - 1)
        meta = jnp.where(lane == j * R + i, dz * tr + (dy * nc + dc) * AGG + far_s[i, 0], meta)
    meta_out[...] = meta

    def share(peer):
        for n in range(3):
            wsend[peer, 0:sl, n * 128:(n + 1) * 128] = wbuf[n, pl.ds(peer * sl, sl), :].astype(bf16)
        lines = jnp.concatenate([near[g, pl.ds(peer * ml, ml), :] for g in range(AGG)], axis=0)
        wsend[peer, sl:sl + near_rows, :] = lines.astype(bf16)

    def one(t):
        peer = lax.rem(j + t, nyc)
        return remote(wsend.at[peer], r1.at[j], s_one.at[t], r_one.at[t], in_plane(peer, x))

    def tell(t):
        return remote(meta_out, meta_in.at[j], s_meta.at[t], r_meta.at[t], in_plane(lax.rem(j + t, nyc), x))

    def send_one(t):
        tell(t).start()
        share(lax.rem(j + t, nyc))
        one(t).start()

    loop(1, nyc, send_one)
    share(j)
    r1[j] = wsend[j]
    meta_in[j] = meta_out[...]

    def wait_one(t):
        tell(t).wait_recv()
        one(t).wait_recv()

    loop(1, nyc, wait_one)

    told = meta_in[0]
    for peer in range(1, nyc):
        told = told + meta_in[peer]
    width = nyc * R
    aimed = lax.broadcasted_iota(i32, (nz * tr, width), 0) == told[0:1, 0:width]
    aimed = jnp.where(aimed, 1.0, 0.0).astype(bf16)
    for m in range(ml):
        lines = jnp.concatenate([r1[peer, m * R:(m + 1) * R, :] for peer in range(nyc)], axis=0)
        summed = jnp.dot(aimed, lines, preferred_element_type=f32).astype(bf16)
        for zt in range(nz):
            zsend[zt, m * tr:(m + 1) * tr, :] = summed[zt * tr:(zt + 1) * tr]

    def two(t):
        return remote(zsend.at[lax.rem(z + t, nz)], r2.at[t], s_two.at[t], r_two.at[t], along_z(t))

    for t in [half] + [t for s in range(half - 1, 0, -1) for t in (s, nz - s)]:
        two(t).start()
    sums = zsend[z].astype(f32)
    for t in [t for s in range(1, half) for t in (s, nz - s)] + [half]:
        two(t).wait_recv()
        sums = sums + r2[t].astype(f32)
    for n in range(3):
        total[n] = sums[:, n * 128:(n + 1) * 128]

    for peer in range(nyc):
        lines = [
            jnp.concatenate([total[n, pl.ds(peer * AGG + g, ml, stride=tr), :] for g in range(AGG)], axis=0)
            for n in range(3)
        ]
        lines = jnp.concatenate(lines, axis=1) + r1[peer, sl:sl + near_rows, :].astype(f32)
        osend[peer] = lines.astype(bf16)

    def three(t):
        q = lax.rem(place + t, group)
        peer = lax.rem(q, nyc)
        return remote(osend.at[peer], r3.at[place], s_three.at[t], r_three.at[t], in_plane(peer, lax.div(q, nyc)))

    loop(1, group, lambda t: three(t).start())
    r3[place] = osend[j]
    loop(1, group, lambda t: three(t).wait_recv())
    for px in range(nx):
        for g in range(AGG):
            lines = [r3[px * nyc + peer].astype(f32)[g * ml:(g + 1) * ml] for peer in range(nyc)]
            out_ref[px * AGG + g] = jnp.concatenate(lines, axis=0).astype(bf16)

    for way in (0, 1):
        for step in range(1, half + 1):
            for piece in order(way, step):
                ring(way, step, piece).wait_send()
    for number in range(half + 1):
        loop(1, nyc, lambda t, number=number: pick_copy(number, t).wait_send())

    def drain(t):
        tell(t).wait_send()
        one(t).wait_send()

    loop(1, nyc, drain)
    loop(1, nz, lambda t: two(t).wait_send())
    loop(1, group, lambda t: three(t).wait_send())


def body(ny, nx, a_blocks, a_nbrs, p_blocks, p_dest, p_far_agg, agg_id, ap_slot, c_slot, send_rows):
    nz = NZ
    half = nz // 2
    nyc = ny * NC
    ml, tr = B // nyc, nyc * AGG
    sl, near_rows = ml * R, ml * AGG
    width = KC * B
    dma = pltpu.SemaphoreType.DMA
    block = lambda *lead: pltpu.VMEM(lead + (B, 128), bf16)
    smem = pl.BlockSpec(memory_space=pltpu.SMEM)
    scratch = [block(R) for _ in range(nz - 1)] + [
        pltpu.VMEM((R, B, KA * B), bf16),
        pltpu.VMEM((nz, 8, 128), i32),
        pltpu.VMEM((nz, 8, 128), i32),
        pltpu.SMEM((nz, 8, 128), i32),
        pltpu.SMEM((R * KA,), i32),
        block(nyc, nz * 2),
        block(R + nyc * nz * 2),
        pltpu.VMEM((3, B * R, 128), f32),
        pltpu.VMEM((AGG, B, width), f32),
        pltpu.VMEM((nyc, sl + near_rows, width), bf16),
        pltpu.VMEM((nyc, sl + near_rows, width), bf16),
        pltpu.VMEM((8, 128), i32),
        pltpu.VMEM((nyc, 8, 128), i32),
        pltpu.VMEM((nz, ml * tr, width), bf16),
        pltpu.VMEM((nz, ml * tr, width), bf16),
        pltpu.VMEM((3, ml * tr, 128), f32),
        pltpu.VMEM((nyc, near_rows, width), bf16),
        pltpu.VMEM((nx * nyc, near_rows, width), bf16),
        dma,
        dma((2, half, R // CHUNK)), dma((2, half, R // CHUNK)),
        dma((nz,)), dma((nz,)), dma,
        dma((half + 1, nyc)), dma((half + 1, nyc)),
        dma((nyc,)), dma((nyc,)), dma((nyc,)), dma((nyc,)),
        dma((nz,)), dma((nz,)),
        dma((nx * nyc,)), dma((nx * nyc,)),
    ]
    return pl.pallas_call(
        functools.partial(kernel, ny, nx),
        out_shape=jax.ShapeDtypeStruct((nx * AGG, B, width), bf16),
        in_specs=[smem] * 7 + [pl.BlockSpec(memory_space=pl.ANY), pl.BlockSpec(memory_space=pltpu.VMEM)],
        out_specs=pl.BlockSpec(memory_space=pltpu.VMEM),
        scratch_shapes=scratch,
        compiler_params=pltpu.CompilerParams(collective_id=0, has_side_effects=True, vmem_limit_bytes=40 * 2**20),
    )(a_nbrs, p_dest, p_far_agg, agg_id, ap_slot, c_slot, send_rows, a_blocks, p_blocks)


def solution(mesh):
    ny = mesh.shape["dom"] // (NZ * NC)
    nx = mesh.shape["sub"]
    both = ("dom", "sub")
    return jax.shard_map(
        functools.partial(body, ny, nx),
        mesh=mesh,
        in_specs=(
            P(both, None, None),
            P(both, None),
            P(both, None, None),
            P(both, None),
            P(both, None),
            P(both, None),
            P(both, None, None),
            P(both, None, None),
            P(both, None),
        ),
        out_specs=P("dom", None, None),
        check_vma=False,
    )
```

time: 669 us -> 105 us (0.16)
  waiting for transfers between devices: 391 us -> 0 us
  other arithmetic: 121 us -> 0 us
  Pallas kernels: 0 us -> 98.6 us
  local copies, waits for them, and re-layouts: 96.2 us -> 6.47 us
  starting transfers between devices: 29.8 us -> 0 us
  matrix products: 15.2 us -> 0 us
  blocking collectives: 11 us -> 0 us
    all_to_all x3 -> x0, waiting for transfers between devices: 391 us -> none  [the longest x1 344 us: body(): lax.all_to_all(to_buffer(contrib[:, 1], 0.0), 'dom', split_axis=0, concat...]
    scatter-add x2 -> x0, other arithmetic: 118 us -> none  [place_blocks(): return coarse_sum.at[targets.reshape(-1)].add(blocks, mode='drop')]
    pallas_call x0 -> x1, Pallas kernels: none -> 98.6 us  [body(): pl.pallas_call(functools.partial(kernel, ny, nx), out_shape=jax.ShapeDtyp...]
    another operation x3 -> x0, local copies, waits for them, and re-layouts: 31.9 us -> none  [place_blocks(): contrib.reshape(item_count, coarse_width, -1, coarse_width)]
    all_to_all x3 -> x0, starting transfers between devices: 29.8 us -> none  [the longest x1 13.3 us: body(): lax.all_to_all(outgoing, 'dom', split_axis=0, concat_axis=0, tiled=True)]
    transpose x1 -> x0, local copies, waits for them, and re-layouts: 27.5 us -> none  [place_blocks(): contrib.reshape(item_count, coarse_width, -1, coarse_width)]
    dot_general x2 -> x0, matrix products: 14.4 us -> none  [the longest x1 10.4 us: body(): jnp.einsum('rkblc,rklq->rbqc', product.reshape(row_count, KA, fine_width,...]
    all_gather x1 -> x0, blocking collectives: 11 us -> none  [body(): return lax.all_gather(coarse, 'sub', axis=0, tiled=True)]
  transfers between devices with their start and end apart: 3 -> 0, of which waited for: 2 -> 0; matrix products, arithmetic and copies ran while one was open for 11% -> 0% of each run, Pallas kernels for 0% -> 0%
where the time goes in v1:
time: 105 us
  Pallas kernels  98.6 us (94%)
  local copies, waits for them, and re-layouts  6.47 us (6%)
    pallas_call x1, Pallas kernels, body(): pl.pallas_call(functools.partial(kernel, ny, nx), out_shape=jax.ShapeDtyp...  98.6 us
    unnamed x23, local copies, waits for them, and re-layouts  6.47 us

profile of v1, /device:TPU:1, one launch (start us, length us, event | category | flops | bytes accessed | tf_op | source)
XLA Modules:
  0.0 105.1 jit_solution(17238870512983104340)
XLA Ops:
  0.0 0.0 copy-start.6
  0.0 0.8 copy.10.nbr_s
  0.8 0.0 copy-done.6
  0.8 0.0 copy-start.7
  0.8 0.0 copy-start.3
  0.8 0.1 copy.11.dest_s
  0.9 0.6 copy-done.7
  1.4 0.1 copy.12.far_s
  1.5 0.0 copy-done.3
  1.5 0.0 copy-start.5
  1.5 0.1 copy.14.cslot_s
  1.6 0.6 copy-done.5
  2.2 0.0 copy-start.4
  2.2 0.1 copy.15.send_s
  2.3 0.6 copy-done.4
  2.9 0.0 copy-start.2
  2.9 0.1 copy.13.slot_s
  3.0 0.5 copy-done.2
  3.6 0.0 copy-start
  3.6 1.2 %copy-done = bf16[16,64,448]{2,1,0:T(8,128)(2,1)S(1)} copy-done((bf16[16,64,448]{2,1,0:T(8,128)(2,1)S(1)}, bf16[16,64,448]{2,1,0:T(8,128)(2,1)}, u32[]{:S(2)}) %copy-start) | copy-done | bytes 917528
  4.8 0.0 copy-start.1
  4.8 0.9 copy-done.1
  5.7 98.6 %shard_map.91 = bf16[8,64,384]{2,1,0:T(8,128)(2,1)S(1)} custom-call(s32[16,6]{1,0:T(8,128)S(1)} %copy.10.nbr_s, s32[16,1]{1,0:T(8,128)S(1)} %copy.11.dest_s, s32[16,1]{1,0:T(8,128)S(1)} %copy.12.far_s, s32[1,16]{1,0:T(1,128)S(1)} %copy-done.2, s32[16,7,2]{2,1,0:T(8,128)S(1)} %copy.13.slot_s, s32[16,2,8]{2,1,0:T(2,128)S(1)} %copy.14.cslot_s, ...), custom_call_target="tpu_custom_call" | custom-call | tf_op jit(solution)/shard_map/pallas_call | solution.py:365
  104.4 0.7 copy.17
Async XLA Ops:
  0.0 0.8 copy-start.6
  0.8 0.7 copy-start.7
  0.8 0.7 copy-start.3
  1.5 0.7 copy-start.5
  2.2 0.7 copy-start.4
  2.9 0.7 copy-start.2
  3.6 1.2 %copy-start = (bf16[16,64,448]{2,1,0:T(8,128)(2,1)S(1)}, bf16[16,64,448]{2,1,0:T(8,128)(2,1)}, u32[]{:S(2)}) copy-start(bf16[16,64,448]{2,1,0:T(8,128)(2,1)} %a_hbm.1) | copy-start | bytes 2752516
  4.8 0.9 copy-start.1

commit v2 on v1

v2 whole, which is shorter than its diff:
```python
import functools

import jax
import jax.numpy as jnp
from jax import lax
from jax.experimental import pallas as pl
from jax.experimental.pallas import tpu as pltpu
from jax.sharding import PartitionSpec as P

MESH = pl.DeviceIdType.MESH
NZ = 8
NC = 2
R = 16
KA = 7
B = 64
AGG = 2
KC = 6
CHUNK = 8
EARLY = 1
WINDOW = 3
f32, bf16, i32 = jnp.float32, jnp.bfloat16, jnp.int32

UNROLL = 4
PARTS = 2


def div(value, size):
    return value >> (size.bit_length() - 1)


def mod(value, size):
    return value & (size - 1)


def kernel(ny, nx, *refs):
    nz, nc = NZ, NC
    half = nz // 2
    nyc = ny * nc
    ml = B // nyc
    tr = nyc * AGG
    mc = ml // PARTS
    sl = mc * R
    near_rows = ml * AGG
    ints, (a_hbm, p_hbm, out_ref), scr = refs[:7], refs[7:10], list(refs[10:])
    int_s = [scr.pop(0) for _ in ints]
    nbr_s, dest_s, far_s, agg_s, slot_s, cslot_s, send_s = int_s
    p_ref, p_sem, int_sem = scr.pop(0), scr.pop(0), scr.pop(0)
    zr = [scr.pop(0) for _ in range(half - 1)]
    zl = [scr.pop(0) for _ in range(half - 1)]
    (zfar, a_vm, idx_out, idx_in, idx_s, cols_s, picks, ext, pt, ap_vm, wbuf, near, wsend, r1, near_in, meta_out, meta_in, dense, two_out, two_in, total, osend, r3,
     a_sem, s_ring, r_ring, s_idx, r_idx, l_idx, s_pick, r_pick, s_one, r_one, s_near, r_near, s_meta, r_meta, s_two, r_two, s_three, r_three) = scr

    dom, x = lax.axis_index("dom"), lax.axis_index("sub")
    y = div(dom, nz * nc)
    z = mod(div(dom, nc), nz)
    c = mod(dom, nc)
    j = y * nc + c
    turn = 1 - 2 * c

    def along_z(step):
        return ((y * nz + mod(z + step + nz, nz)) * nc + c, x)

    def in_plane(peer, px):
        return ((div(peer, nc) * nz + z) * nc + mod(peer, nc), px)

    def remote(src, dst, send, recv, device):
        return pltpu.make_async_remote_copy(
            src_ref=src, dst_ref=dst, send_sem=send, recv_sem=recv, device_id=device, device_id_type=MESH
        )

    def loop(lo, hi, fn):
        lax.fori_loop(lo, hi, lambda t, carry: (fn(t), carry)[1], 0)

    barrier = pltpu.get_barrier_semaphore()
    group = nx * nyc
    place = x * nyc + j
    int_copies = [pltpu.make_async_copy(src, dst, int_sem.at[n]) for n, (src, dst) in enumerate(zip(ints, int_s))]
    for copy in int_copies[::-1]:
        copy.start()
    p_copy = pltpu.make_async_copy(p_hbm, p_ref, p_sem)
    p_copy.start()
    loop(1, nz, lambda t: pl.semaphore_signal(barrier, inc=1, device_id=along_z(t), device_id_type=MESH))

    def greet(t):
        q = mod(place + t, group)
        pl.semaphore_signal(barrier, inc=1, device_id=in_plane(mod(q, nyc), div(q, nyc)), device_id_type=MESH)

    loop(1, group, greet)
    a_copy = pltpu.make_async_copy(a_hbm, a_vm, a_sem)
    a_copy.start()
    p_copy.wait()
    pl.semaphore_wait(barrier, nz - 1 + group - 1)

    def ring(way, step, piece):
        there = (zr, zl)[way]
        src = p_ref if step == 1 else there[step - 2]
        dst = there[step - 1] if step < half else zfar
        rows = pl.ds(piece * CHUNK, CHUNK)
        return remote(
            src.at[rows], dst.at[rows], s_ring.at[way, step - 1, piece], r_ring.at[way, step - 1, piece],
            along_z(turn if way == 0 else -turn),
        )

    pieces = R // CHUNK

    def order(way, step):
        listed = list(range(pieces)) if way == 0 else list(range(pieces))[::-1]
        return listed if step < half else listed[: pieces // 2]

    blocks = [(way, step) for step in range(1, half + 1) for way in (0, 1)]
    plan = [(way, step, piece) for way, step in blocks for piece in order(way, step)]
    begun = []

    def begin():
        if len(begun) >= WINDOW:
            ring(*plan[len(begun) - WINDOW]).wait_send()
        begun.append(plan[len(begun)])
        ring(*begun[-1]).start()

    for n in range(EARLY):
        begin()

    for copy in int_copies:
        copy.wait()

    lane = lax.broadcasted_iota(i32, (8, 128), 1)

    def list_for(t):
        zt = mod(z + turn * t + nz, nz)
        tile = jnp.zeros((8, 128), i32)
        for peer in range(nyc):
            for f in range(2):
                row = send_s[f, ((peer // nc) * nz + zt) * nc + peer % nc]
                tile = jnp.where(lane == peer * 2 + f, row, tile)
        return tile

    def slot_of(t):
        return 0 if t == 0 else 2 * t - 1 if t < half else nz - 1 if t == half else 2 * (nz - t)

    idx_in[0] = list_for(0)
    for t in range(1, nz):
        idx_out[t] = list_for(t)

    index_copies = [
        remote(idx_out.at[t], idx_in.at[slot_of(t)], s_idx.at[t], r_idx.at[t], along_z(turn * t)) for t in range(1, nz)
    ]
    for copy in index_copies:
        copy.start()
    while len(begun) < WINDOW:
        begin()

    def pick_copy(slot, t):
        return remote(
            picks.at[t, pl.ds(slot * 2, 2)], ext.at[pl.ds(R + (j * nz + slot) * 2, 2)],
            s_pick.at[slot, t], r_pick.at[slot, t], in_plane(mod(j + t, nyc), x),
        )

    def pick(slot, source, index):
        for f in range(2):
            ext[R + (j * nz + slot) * 2 + f] = source[index(j, f)]

        def for_peer(t):
            peer = mod(j + t, nyc)
            for f in range(2):
                picks[t, slot * 2 + f] = source[index(peer, f)]
            pick_copy(slot, t).start()

        loop(1, nyc, for_peer)

    pick(0, p_ref, lambda peer, f: send_s[f, (div(peer, nc) * nz + z) * nc + mod(peer, nc)])
    def place_row(i):
        cols_s[i * KA] = i
        for k in range(1, KA):
            n = nbr_s[k - 1, i]
            e = n - R
            f = e & 1
            owner = e >> 1
            oc = owner & (nc - 1)
            oz = (owner >> (nc.bit_length() - 1)) & (nz - 1)
            oy = owner >> ((nz * nc).bit_length() - 1)
            dz = (jnp.where(oc == 0, oz - z, z - oz) + nz) & (nz - 1)
            slot = jnp.where(dz == half, nz - 1, jnp.where(dz < half, 2 * dz, 2 * (nz - dz) - 1))
            cols_s[i * KA + k] = jnp.where(n < R, n, R + ((oy * nc + oc) * nz + slot) * 2 + f)

    def pick_block(way, step):
        if (way, step) == (0, 1):
            for copy in index_copies:
                copy.wait()
            to_scalars = pltpu.make_async_copy(idx_in, idx_s, l_idx)
            to_scalars.start()
            to_scalars.wait()
        slot = 2 * step - 1 + way if step < half else nz - 1
        pick(slot, (zr, zl)[way][step - 1] if step < half else zfar, lambda peer, f: idx_s[slot, 0, peer * 2 + f])

    line = lax.broadcasted_iota(i32, (2 * B, 128), 0)
    part, share_of, rest = div(line, nyc * mc), mod(div(line, mc), nyc), mod(line, mc)
    source = jnp.where(line < B, B + share_of * ml + part * mc + rest, line - B)
    reorder = jnp.where(lax.broadcasted_iota(i32, (2 * B, 128), 1) == source, 1.0, 0.0).astype(bf16)

    def transpose(i):
        pt[i] = lax.dot_general(reorder, p_ref[i], (((1,), (1,)), ((), ())), preferred_element_type=f32).astype(bf16)

    for way, step in blocks:
        listed = order(way, step)
        for piece in listed:
            if step > 1:
                ring(way, step - 1, piece).wait_recv()
                if piece == listed[-1]:
                    for other in order(way, step - 1):
                        if other not in listed:
                            ring(way, step - 1, other).wait_recv()
                    pick_block(way, step - 1)
            if (way, step, piece) not in plan[:WINDOW]:
                begin()
    for way in (0, 1):
        for piece in order(way, half):
            ring(way, half, piece).wait_recv()
    pick_block(0, half)
    loop(0, R, place_row)
    ext[0:R] = p_ref[...]
    lax.fori_loop(0, R, lambda t, carry: (transpose(t), carry)[1], 0, unroll=4)
    for slot in range(nz):
        loop(1, nyc, lambda t, slot=slot: pick_copy(slot, t).wait_recv())
    a_copy.wait()

    lane1 = lax.broadcasted_iota(i32, (1, 128), 1)
    low = lane1 < B
    high = jnp.where(low, 0, 1)
    low_mask = jnp.where(low, 1.0, 0.0).astype(bf16)
    high_mask = jnp.where(low, 0.0, 1.0).astype(bf16)
    near[...] = jnp.zeros_like(near)

    def masks(s0, s1, pairs):
        same = jnp.where(low, s0, s1) - high
        cross = jnp.where(low, s1, s0) - high
        return [
            (jnp.where(same == 2 * q, 1.0, 0.0).astype(f32), jnp.where(cross == 2 * q, 1.0, 0.0).astype(f32))
            for q in range(pairs)
        ]

    def row(i):
        ap = [None] * 4

        def merge(k, q):
            turned = pltpu.roll(q, B, 1)
            for n, (same, cross) in enumerate(masks(slot_s[k, 0, i], slot_s[k, 1, i], 4)):
                term = q * same + turned * cross
                ap[n] = term if ap[n] is None else ap[n] + term

        for pair in range(KA // 2):
            a = a_vm[i, :, pair * 128:(pair + 1) * 128]
            left = jnp.concatenate([a * low_mask, a * high_mask], axis=0)
            right = jnp.concatenate([ext[cols_s[i * KA + 2 * pair]], ext[cols_s[i * KA + 2 * pair + 1]]], axis=0)
            q = jnp.dot(left, right, preferred_element_type=f32)
            merge(2 * pair, q[:B])
            merge(2 * pair + 1, q[B:])
        q = jnp.dot(a_vm[i, :, (KA - 1) * B:], ext[cols_s[i * KA + KA - 1]], preferred_element_type=f32)
        merge(KA - 1, q)
        ap_vm[i] = jnp.concatenate([block.astype(bf16) for block in ap], axis=1)

    def rows(fn):
        lax.fori_loop(0, R, lambda t, carry: (fn(t), carry)[1], 0, unroll=UNROLL)

    rows(row)

    def coarse_row(i, m, lines):
        w = jnp.dot(lines, ap_vm[i], preferred_element_type=f32)
        to = [None] * 3
        for q in range(4):
            block = w[:, q * 128:(q + 1) * 128]
            turned = pltpu.roll(block, B, 1)
            for n, (same, cross) in enumerate(masks(cslot_s[m, 2 * q, i], cslot_s[m, 2 * q + 1, i], 3)):
                term = block * same + turned * cross
                to[n] = term if to[n] is None else to[n] + term
        return to

    meta = jnp.zeros((8, 128), i32)
    for i in range(R):
        d = dest_s[0, i]
        dc = d & (nc - 1)
        dz = (d >> (nc.bit_length() - 1)) & (nz - 1)
        dy = d >> ((nz * nc).bit_length() - 1)
        meta = jnp.where(lane == j * R + i, dz * tr + (dy * nc + dc) * AGG + far_s[0, i], meta)
    meta_out[...] = meta

    def share(part, peer):
        for n in range(3):
            wsend[part, peer, :, n * 128:(n + 1) * 128] = wbuf[part, n, pl.ds(peer * sl, sl), :].astype(bf16)

    def one(part, t):
        peer = mod(j + t, nyc)
        return remote(wsend.at[part, peer], r1.at[part, j], s_one.at[part, t], r_one.at[part, t], in_plane(peer, x))

    def tell(t):
        return remote(meta_out, meta_in.at[j], s_meta.at[t], r_meta.at[t], in_plane(mod(j + t, nyc), x))

    def send_near(t):
        return remote(near, near_in.at[x], s_near.at[t], r_near.at[t], (dom, mod(x + t, nx)))

    loop(1, nyc, lambda t: tell(t).start())
    meta_in[j] = meta_out[...]
    for part in range(PARTS):
        def far_row(i, part=part):
            for n, lines in enumerate(coarse_row(i, 1, pt[i, part * nyc * mc:(part + 1) * nyc * mc, :])):
                wbuf[part, n, pl.ds(i, nyc * mc, stride=R), :] = lines

        rows(far_row)

        def send_one(t, part=part):
            share(part, mod(j + t, nyc))
            one(part, t).start()

        loop(1, nyc, send_one)
        share(part, j)
        r1[part, j] = wsend[part, j]

    def near_row(i):
        agg = agg_s[0, i]
        for n, lines in enumerate(coarse_row(i, 0, pt[i, B:2 * B, :])):
            for g in range(AGG):
                near[g, :, n * 128:(n + 1) * 128] += lines * jnp.where(agg == g, 1.0, 0.0).astype(f32)

    rows(near_row)

    loop(1, nx, lambda t: send_near(t).start())
    near_in[x] = near[...]

    loop(1, nyc, lambda t: tell(t).wait_recv())
    told = meta_in[0]
    for peer in range(1, nyc):
        told = told + meta_in[peer]
    width = nyc * R
    aimed = lax.broadcasted_iota(i32, (nz * tr, width), 0) == told[0:1, 0:width]
    aimed = jnp.where(aimed, 1.0, 0.0).astype(bf16)

    deep = mc * tr
    cut = deep // 2

    def two(part, way, step):
        rows = pl.ds(way * cut, cut) if step == 1 else pl.ds(0, deep)
        return remote(
            two_out.at[part, way, step - 1, rows], two_in.at[part, way, step - 1, rows],
            s_two.at[part, way, step - 1], r_two.at[part, way, step - 1], along_z(1 - 2 * way),
        )

    def pass_on(part, step):
        for way in (0, 1):
            own = dense.at[part, mod(z + (1 - 2 * way) * (half - step + 1) + nz, nz)]
            out = two_out.at[part, way, step - 1]
            if step > 1:
                two(part, way, step - 1).wait_recv()
            for first in (0, cut):
                rows = slice(first, first + cut)
                if step == 1 and first != way * cut:
                    continue
                value = own[rows]
                if step > 2 or (step == 2 and first == way * cut):
                    value = value + two_in[part, way, step - 2, rows].astype(f32)
                out[rows] = value.astype(bf16)
            two(part, way, step).start()

    def finish(part):
        sums = dense[part, z]
        for way in (0, 1):
            two(part, way, half).wait_recv()
            sums = sums + two_in[part, way, half - 1].astype(f32)
        for n in range(3):
            total[n, part * deep:(part + 1) * deep, :] = sums[:, n * 128:(n + 1) * 128]

    for turn_of in range(PARTS + half):
        if turn_of < PARTS:
            part = turn_of
            loop(1, nyc, lambda t, part=part: one(part, t).wait_recv())
            for m in range(mc):
                lines = jnp.concatenate([r1[part, peer, m * R:(m + 1) * R, :] for peer in range(nyc)], axis=0)
                summed = jnp.dot(aimed, lines, preferred_element_type=f32)
                for zt in range(nz):
                    dense[part, zt, m * tr:(m + 1) * tr, :] = summed[zt * tr:(zt + 1) * tr]
        for part in range(max(0, turn_of - half), min(PARTS, turn_of + 1)):
            step = turn_of - part + 1
            if step <= half:
                pass_on(part, step)
            else:
                finish(part)

    for peer in range(nyc):
        lines = [
            jnp.concatenate([total[n, pl.ds(peer * AGG + g, ml, stride=tr), :] for g in range(AGG)], axis=0)
            for n in range(3)
        ]
        osend[peer] = jnp.concatenate(lines, axis=1).astype(bf16)

    def three(t):
        q = mod(place + t, group)
        peer = mod(q, nyc)
        return remote(osend.at[peer], r3.at[place], s_three.at[t], r_three.at[t], in_plane(peer, div(q, nyc)))

    loop(1, group, lambda t: three(t).start())
    r3[place] = osend[j]
    loop(1, nx, lambda t: send_near(t).wait_recv())
    loop(1, group, lambda t: three(t).wait_recv())
    for px in range(nx):
        for g in range(AGG):
            lines = [r3[px * nyc + peer].astype(f32)[g * ml:(g + 1) * ml] for peer in range(nyc)]
            out_ref[px * AGG + g] = (jnp.concatenate(lines, axis=0) + near_in[px, g]).astype(bf16)

    for item in plan[len(plan) - WINDOW:]:
        ring(*item).wait_send()
    for slot in range(nz):
        loop(1, nyc, lambda t, slot=slot: pick_copy(slot, t).wait_send())

    def drain(t):
        tell(t).wait_send()
        for part in range(PARTS):
            one(part, t).wait_send()

    loop(1, nyc, drain)
    loop(1, nx, lambda t: send_near(t).wait_send())
    for part in range(PARTS):
        for way in (0, 1):
            for step in range(1, half + 1):
                two(part, way, step).wait_send()
    loop(1, group, lambda t: three(t).wait_send())


def body(ny, nx, a_blocks, a_nbrs, p_blocks, p_dest, p_far_agg, agg_id, ap_slot, c_slot, send_rows):
    nz = NZ
    half = nz // 2
    nyc = ny * NC
    ml, tr = B // nyc, nyc * AGG
    mc = ml // PARTS
    sl, near_rows = mc * R, ml * AGG
    width = KC * B
    dma = pltpu.SemaphoreType.DMA
    block = lambda *lead: pltpu.VMEM(lead + (B, 128), bf16)
    ints = (a_nbrs.T, p_dest.T, p_far_agg.T, agg_id, ap_slot.transpose(1, 2, 0), c_slot.transpose(1, 2, 0), send_rows.T)
    scratch = [pltpu.SMEM(array.shape, i32) for array in ints] + [block(R), dma, dma((len(ints),))]
    scratch += [block(R) for _ in range(nz - 1)] + [
        pltpu.VMEM((R, B, KA * B), bf16),
        pltpu.VMEM((nz, 8, 128), i32),
        pltpu.VMEM((nz, 8, 128), i32),
        pltpu.SMEM((nz, 8, 128), i32),
        pltpu.SMEM((R * KA,), i32),
        block(nyc, nz * 2),
        block(R + nyc * nz * 2),
        pltpu.VMEM((R, 2 * B, B), bf16),
        pltpu.VMEM((R, B, 4 * 128), bf16),
        pltpu.VMEM((PARTS, 3, nyc * sl, 128), f32),
        pltpu.VMEM((AGG, B, width), f32),
        pltpu.VMEM((PARTS, nyc, sl, width), bf16),
        pltpu.VMEM((PARTS, nyc, sl, width), bf16),
        pltpu.VMEM((nx, AGG, B, width), f32),
        pltpu.VMEM((8, 128), i32),
        pltpu.VMEM((nyc, 8, 128), i32),
        pltpu.VMEM((PARTS, nz, mc * tr, width), f32),
        pltpu.VMEM((PARTS, 2, half, mc * tr, width), bf16),
        pltpu.VMEM((PARTS, 2, half, mc * tr, width), bf16),
        pltpu.VMEM((3, ml * tr, 128), f32),
        pltpu.VMEM((nyc, near_rows, width), bf16),
        pltpu.VMEM((nx * nyc, near_rows, width), bf16),
        dma,
        dma((2, half, R // CHUNK)), dma((2, half, R // CHUNK)),
        dma((nz,)), dma((nz,)), dma,
        dma((nz, nyc)), dma((nz, nyc)),
        dma((PARTS, nyc)), dma((PARTS, nyc)), dma((nyc,)), dma((nyc,)), dma((nyc,)), dma((nyc,)),
        dma((PARTS, 2, half)), dma((PARTS, 2, half)),
        dma((nx * nyc,)), dma((nx * nyc,)),
    ]
    return pl.pallas_call(
        functools.partial(kernel, ny, nx),
        out_shape=jax.ShapeDtypeStruct((nx * AGG, B, width), bf16),
        in_specs=[pl.BlockSpec(memory_space=pl.ANY)] * (len(ints) + 2),
        out_specs=pl.BlockSpec(memory_space=pltpu.VMEM),
        scratch_shapes=scratch,
        compiler_params=pltpu.CompilerParams(collective_id=0, has_side_effects=True, vmem_limit_bytes=62 * 2**20),
    )(*ints, a_blocks, p_blocks)


def solution(mesh):
    ny = mesh.shape["dom"] // (NZ * NC)
    nx = mesh.shape["sub"]
    both = ("dom", "sub")
    return jax.shard_map(
        functools.partial(body, ny, nx),
        mesh=mesh,
        in_specs=(
            P(both, None, None),
            P(both, None),
            P(both, None, None),
            P(both, None),
            P(both, None),
            P(both, None),
            P(both, None, None),
            P(both, None, None),
            P(both, None),
        ),
        out_specs=P("dom", None, None),
        check_vma=False,
    )
```

time: 105 us -> 85.8 us (0.82)
  Pallas kernels: 98.6 us -> 83.9 us
  local copies, waits for them, and re-layouts: 6.47 us -> 1.78 us
    pallas_call x1, Pallas kernels: 98.6 us -> 83.9 us  [body(): pl.pallas_call(functools.partial(kernel, ny, nx), out_shape=jax.ShapeDtyp...]
    unnamed x23 -> x1, local copies, waits for them, and re-layouts: 6.47 us -> 1.78 us
where the time goes in v2:
time: 85.8 us; the launch traced here: 85.6 us
  Pallas kernels  83.9 us (98%)
  local copies, waits for them, and re-layouts  1.78 us (2%)
    pallas_call x1, Pallas kernels, body(): pl.pallas_call(functools.partial(kernel, ny, nx), out_shape=jax.ShapeDtyp...  83.9 us
    unnamed x1, local copies, waits for them, and re-layouts  1.78 us

profile of v2, /device:TPU:1, one launch (start us, length us, event | category | flops | bytes accessed | tf_op | source)
XLA Modules:
  0.0 85.6 jit_solution(4543829388141876921)
XLA Ops:
  0.0 83.9 %shard_map.91 = bf16[8,64,384]{2,1,0:T(8,128)(2,1)} custom-call(s32[6,16]{1,0:T(8,128)} %bitcast.8, s32[1,16]{1,0:T(1,128)} %bitcast.10, s32[1,16]{1,0:T(1,128)} %bitcast.11, s32[1,16]{1,0:T(1,128)} %refs_3_.1, s32[7,2,16]{2,1,0:T(2,128)} %bitcast.7, s32[2,8,16]{2,1,0:T(8,128)} %bitcast.6, s32[2,64]{1,0:T(2,128)} %bitcast.9, bf16[16,64,448]{2,1,0:T(8,128)(2,1)} %refs_7_.1, ...), custom_call_target="tpu_custom_call" | custom-call | tf_op jit(solution)/shard_map/pallas_call | solution.py:469
  83.9 1.8 %copy.11 = bf16[8,64,384]{2,1,0:T(8,128)(2,1)} copy(bf16[8,64,384]{2,1,0:T(8,128)(2,1)} %shard_map.91) | data formatting | bytes 786432

commit v3 on v2

--- a/solution.py
+++ b/solution.py
@@ -17,10 +17,9 @@
 KC = 6
 CHUNK = 8
 EARLY = 1
-WINDOW = 3
 f32, bf16, i32 = jnp.float32, jnp.bfloat16, jnp.int32
 
-UNROLL = 4
+UNROLL = 8
 PARTS = 2
 
 
@@ -112,8 +111,6 @@
     begun = []
 
     def begin():
-        if len(begun) >= WINDOW:
-            ring(*plan[len(begun) - WINDOW]).wait_send()
         begun.append(plan[len(begun)])
         ring(*begun[-1]).start()
 
@@ -146,7 +143,7 @@
     ]
     for copy in index_copies:
         copy.start()
-    while len(begun) < WINDOW:
+    while len(begun) < 2 * pieces:
         begin()
 
     def pick_copy(slot, t):
@@ -210,12 +207,25 @@
                         if other not in listed:
                             ring(way, step - 1, other).wait_recv()
                     pick_block(way, step - 1)
-            if (way, step, piece) not in plan[:WINDOW]:
                 begin()
     for way in (0, 1):
         for piece in order(way, half):
             ring(way, half, piece).wait_recv()
     pick_block(0, half)
+    meta = jnp.zeros((8, 128), i32)
+    for i in range(R):
+        d = dest_s[0, i]
+        dc = d & (nc - 1)
+        dz = (d >> (nc.bit_length() - 1)) & (nz - 1)
+        dy = d >> ((nz * nc).bit_length() - 1)
+        meta = jnp.where(lane == j * R + i, dz * tr + (dy * nc + dc) * AGG + far_s[0, i], meta)
+    meta_out[...] = meta
+
+    def tell(t):
+        return remote(meta_out, meta_in.at[j], s_meta.at[t], r_meta.at[t], in_plane(mod(j + t, nyc), x))
+
+    loop(1, nyc, lambda t: tell(t).start())
+    meta_in[j] = meta_out[...]
     loop(0, R, place_row)
     ext[0:R] = p_ref[...]
     lax.fori_loop(0, R, lambda t, carry: (transpose(t), carry)[1], 0, unroll=4)
@@ -261,8 +271,6 @@
     def rows(fn):
         lax.fori_loop(0, R, lambda t, carry: (fn(t), carry)[1], 0, unroll=UNROLL)
 
-    rows(row)
-
     def coarse_row(i, m, lines):
         w = jnp.dot(lines, ap_vm[i], preferred_element_type=f32)
         to = [None] * 3
@@ -274,15 +282,6 @@
                 to[n] = term if to[n] is None else to[n] + term
         return to
 
-    meta = jnp.zeros((8, 128), i32)
-    for i in range(R):
-        d = dest_s[0, i]
-        dc = d & (nc - 1)
-        dz = (d >> (nc.bit_length() - 1)) & (nz - 1)
-        dy = d >> ((nz * nc).bit_length() - 1)
-        meta = jnp.where(lane == j * R + i, dz * tr + (dy * nc + dc) * AGG + far_s[0, i], meta)
-    meta_out[...] = meta
-
     def share(part, peer):
         for n in range(3):
             wsend[part, peer, :, n * 128:(n + 1) * 128] = wbuf[part, n, pl.ds(peer * sl, sl), :].astype(bf16)
@@ -291,14 +290,10 @@
         peer = mod(j + t, nyc)
         return remote(wsend.at[part, peer], r1.at[part, j], s_one.at[part, t], r_one.at[part, t], in_plane(peer, x))
 
-    def tell(t):
-        return remote(meta_out, meta_in.at[j], s_meta.at[t], r_meta.at[t], in_plane(mod(j + t, nyc), x))
-
     def send_near(t):
         return remote(near, near_in.at[x], s_near.at[t], r_near.at[t], (dom, mod(x + t, nx)))
 
-    loop(1, nyc, lambda t: tell(t).start())
-    meta_in[j] = meta_out[...]
+    rows(row)
     for part in range(PARTS):
         def far_row(i, part=part):
             for n, lines in enumerate(coarse_row(i, 1, pt[i, part * nyc * mc:(part + 1) * nyc * mc, :])):
@@ -367,21 +362,21 @@
         for n in range(3):
             total[n, part * deep:(part + 1) * deep, :] = sums[:, n * 128:(n + 1) * 128]
 
-    for turn_of in range(PARTS + half):
-        if turn_of < PARTS:
-            part = turn_of
-            loop(1, nyc, lambda t, part=part: one(part, t).wait_recv())
-            for m in range(mc):
-                lines = jnp.concatenate([r1[part, peer, m * R:(m + 1) * R, :] for peer in range(nyc)], axis=0)
-                summed = jnp.dot(aimed, lines, preferred_element_type=f32)
-                for zt in range(nz):
-                    dense[part, zt, m * tr:(m + 1) * tr, :] = summed[zt * tr:(zt + 1) * tr]
-        for part in range(max(0, turn_of - half), min(PARTS, turn_of + 1)):
-            step = turn_of - part + 1
-            if step <= half:
-                pass_on(part, step)
-            else:
-                finish(part)
+    def merge_part(part):
+        loop(1, nyc, lambda t: one(part, t).wait_recv())
+        for m in range(mc):
+            lines = jnp.concatenate([r1[part, peer, m * R:(m + 1) * R, :] for peer in range(nyc)], axis=0)
+            summed = jnp.dot(aimed, lines, preferred_element_type=f32)
+            for zt in range(nz):
+                dense[part, zt, m * tr:(m + 1) * tr, :] = summed[zt * tr:(zt + 1) * tr]
+
+    for step, part in [(step, part) for step in range(half + 2) for part in range(PARTS)]:
+        if step == 0:
+            merge_part(part)
+        elif step <= half:
+            pass_on(part, step)
+        else:
+            finish(part)
 
     for peer in range(nyc):
         lines = [
@@ -397,14 +392,8 @@
 
     loop(1, group, lambda t: three(t).start())
     r3[place] = osend[j]
-    loop(1, nx, lambda t: send_near(t).wait_recv())
-    loop(1, group, lambda t: three(t).wait_recv())
-    for px in range(nx):
-        for g in range(AGG):
-            lines = [r3[px * nyc + peer].astype(f32)[g * ml:(g + 1) * ml] for peer in range(nyc)]
-            out_ref[px * AGG + g] = (jnp.concatenate(lines, axis=0) + near_in[px, g]).astype(bf16)
-
-    for item in plan[len(plan) - WINDOW:]:
+
+    for item in plan:
         ring(*item).wait_send()
     for slot in range(nz):
         loop(1, nyc, lambda t, slot=slot: pick_copy(slot, t).wait_send())
@@ -421,6 +410,13 @@
             for step in range(1, half + 1):
                 two(part, way, step).wait_send()
     loop(1, group, lambda t: three(t).wait_send())
+
+    loop(1, nx, lambda t: send_near(t).wait_recv())
+    loop(1, group, lambda t: three(t).wait_recv())
+    for px in range(nx):
+        for g in range(AGG):
+            lines = [r3[px * nyc + peer].astype(f32)[g * ml:(g + 1) * ml] for peer in range(nyc)]
+            out_ref[px * AGG + g] = (jnp.concatenate(lines, axis=0) + near_in[px, g]).astype(bf16)
 
 
 def body(ny, nx, a_blocks, a_nbrs, p_blocks, p_dest, p_far_agg, agg_id, ap_slot, c_slot, send_rows):

time: 85.8 us -> 83.9 us (0.978)
  Pallas kernels: 83.9 us -> 82 us
    pallas_call x1, Pallas kernels: 83.9 us -> 82 us  [body(): pl.pallas_call(functools.partial(kernel, ny, nx), out_shape=jax.ShapeDtyp...]
where the time goes in v3:
time: 83.9 us; the launch traced here: 83.8 us
  Pallas kernels  82 us (98%)
  local copies, waits for them, and re-layouts  1.78 us (2%)
    pallas_call x1, Pallas kernels, body(): pl.pallas_call(functools.partial(kernel, ny, nx), out_shape=jax.ShapeDtyp...  82 us
    unnamed x1, local copies, waits for them, and re-layouts  1.78 us

profile of v3, /device:TPU:1, one launch (start us, length us, event | category | flops | bytes accessed | tf_op | source)
XLA Modules:
  0.0 83.8 jit_solution(17497014630623919113)
XLA Ops:
  0.0 82.0 %shard_map.91 = bf16[8,64,384]{2,1,0:T(8,128)(2,1)} custom-call(s32[6,16]{1,0:T(8,128)} %bitcast.8, s32[1,16]{1,0:T(1,128)} %bitcast.10, s32[1,16]{1,0:T(1,128)} %bitcast.11, s32[1,16]{1,0:T(1,128)} %refs_3_.1, s32[7,2,16]{2,1,0:T(2,128)} %bitcast.7, s32[2,8,16]{2,1,0:T(8,128)} %bitcast.6, s32[2,64]{1,0:T(2,128)} %bitcast.9, bf16[16,64,448]{2,1,0:T(8,128)(2,1)} %refs_7_.1, ...), custom_call_target="tpu_custom_call" | custom-call | tf_op jit(solution)/shard_map/pallas_call | solution.py:465
  82.0 1.8 %copy.11 = bf16[8,64,384]{2,1,0:T(8,128)(2,1)} copy(bf16[8,64,384]{2,1,0:T(8,128)(2,1)} %shard_map.91) | data formatting | bytes 786432

commit v4 on v3

--- a/solution.py
+++ b/solution.py
@@ -249,24 +249,25 @@
         ]
 
     def row(i):
-        ap = [None] * 4
-
-        def merge(k, q):
-            turned = pltpu.roll(q, B, 1)
-            for n, (same, cross) in enumerate(masks(slot_s[k, 0, i], slot_s[k, 1, i], 4)):
-                term = q * same + turned * cross
-                ap[n] = term if ap[n] is None else ap[n] + term
-
+        def placed(k):
+            block = ext[cols_s[i * KA + k]]
+            turned = jnp.concatenate([block[:, B:], block[:, :B]], axis=1)
+            pairs = masks(slot_s[k, 0, i], slot_s[k, 1, i], 4)
+            return (
+                jnp.concatenate([block * same.astype(bf16) for same, _ in pairs], axis=1),
+                jnp.concatenate([turned * cross.astype(bf16) for _, cross in pairs], axis=1),
+            )
+
+        left, right = [], []
         for pair in range(KA // 2):
-            a = a_vm[i, :, pair * 128:(pair + 1) * 128]
-            left = jnp.concatenate([a * low_mask, a * high_mask], axis=0)
-            right = jnp.concatenate([ext[cols_s[i * KA + 2 * pair]], ext[cols_s[i * KA + 2 * pair + 1]]], axis=0)
-            q = jnp.dot(left, right, preferred_element_type=f32)
-            merge(2 * pair, q[:B])
-            merge(2 * pair + 1, q[B:])
-        q = jnp.dot(a_vm[i, :, (KA - 1) * B:], ext[cols_s[i * KA + KA - 1]], preferred_element_type=f32)
-        merge(KA - 1, q)
-        ap_vm[i] = jnp.concatenate([block.astype(bf16) for block in ap], axis=1)
+            first, second = placed(2 * pair), placed(2 * pair + 1)
+            left += [a_vm[i, :, pair * 128:(pair + 1) * 128]] * 2
+            right += [first[0], second[0], first[1], second[1]]
+        ap = jnp.dot(jnp.concatenate(left, axis=1), jnp.concatenate(right, axis=0), preferred_element_type=f32)
+        last = a_vm[i, :, (KA - 1) * B:]
+        for block in placed(KA - 1):
+            ap = ap + jnp.dot(last, block, preferred_element_type=f32)
+        ap_vm[i] = ap.astype(bf16)
 
     def rows(fn):
         lax.fori_loop(0, R, lambda t, carry: (fn(t), carry)[1], 0, unroll=UNROLL)

time: 83.9 us -> 84.1 us (level)
  no operation moved by 1% of the time
where the time goes in v4:
time: 84.1 us; the launch traced here: 83.9 us
  Pallas kernels  82.1 us (98%)
  local copies, waits for them, and re-layouts  1.78 us (2%)
    pallas_call x1, Pallas kernels, body(): pl.pallas_call(functools.partial(kernel, ny, nx), out_shape=jax.ShapeDtyp...  82.1 us
    unnamed x1, local copies, waits for them, and re-layouts  1.78 us

profile of v4, /device:TPU:1, one launch (start us, length us, event | category | flops | bytes accessed | tf_op | source)
XLA Modules:
  0.0 83.9 jit_solution(8066412143580563184)
XLA Ops:
  0.0 82.1 %shard_map.91 = bf16[8,64,384]{2,1,0:T(8,128)(2,1)} custom-call(s32[6,16]{1,0:T(8,128)} %bitcast.8, s32[1,16]{1,0:T(1,128)} %bitcast.10, s32[1,16]{1,0:T(1,128)} %bitcast.11, s32[1,16]{1,0:T(1,128)} %refs_3_.1, s32[7,2,16]{2,1,0:T(2,128)} %bitcast.7, s32[2,8,16]{2,1,0:T(8,128)} %bitcast.6, s32[2,64]{1,0:T(2,128)} %bitcast.9, bf16[16,64,448]{2,1,0:T(8,128)(2,1)} %refs_7_.1, ...), custom_call_target="tpu_custom_call" | custom-call | tf_op jit(solution)/shard_map/pallas_call | solution.py:466
  82.2 1.8 %copy.11 = bf16[8,64,384]{2,1,0:T(8,128)(2,1)} copy(bf16[8,64,384]{2,1,0:T(8,128)(2,1)} %shard_map.91) | data formatting | bytes 786432
